TPU v7x, 32 devices: a whole 2x2x4 slice. The times are simulated.
32 devices in a mesh: dp: 4 (over z), emb: 8 (over y, x, core).
Axes of the slice: x: 2, y: 2, z: 4, core: 2. Of those that a mesh axis runs over, the one named last changes fastest.
Arguments:
- pixels: bfloat16 [32768, 768], P(('dp', 'emb')), may hold values from -6 to 6
- counts: int32 [32, 2], P(('dp', 'emb')), may hold values from 0 to 511, as said below
- token_ids: int32 [32768], P(('dp', 'emb')), may hold values from 0 to 31999, as said below
- action_bins: int32 [32768], P(('dp', 'emb')), may hold values from 0 to 1023
- patch_pos: int32 [32768], P(('dp', 'emb')), may hold values from 0 to 255
- token_table: bfloat16 [33024, 768], P('emb'), may hold values from -6 to 6
- pos_table: bfloat16 [256, 768], replicated, may hold values from -4 to 4
- w_patch: bfloat16 [768, 768], replicated, may hold values from -0.21875 to 0.21875
- w_res_a: bfloat16 [768, 768], replicated, may hold values from -0.21875 to 0.21875
- w_res_b: bfloat16 [768, 768], replicated, may hold values from -0.21875 to 0.21875
- gain_one: bfloat16 [768], replicated, may hold values from 0.5 to 1.5
- bias_one: bfloat16 [768], replicated, may hold values from -2 to 2
- w_q: bfloat16 [768, 768], replicated, may hold values from -0.21875 to 0.21875
- w_k: bfloat16 [768, 768], replicated, may hold values from -0.21875 to 0.21875
- w_v: bfloat16 [768, 768], replicated, may hold values from -0.21875 to 0.21875
- w_o: bfloat16 [768, 768], replicated, may hold values from -1 to 1
- gain_two: bfloat16 [768], replicated, may hold values from 0.5 to 1.5
- bias_two: bfloat16 [768], replicated, may hold values from -2 to 2
- w_up: bfloat16 [768, 3072], replicated, may hold values from -0.21875 to 0.21875
- w_down: bfloat16 [3072, 768], replicated, may hold values from -0.109375 to 0.109375
- cotangent: bfloat16 [32768, 768], P(('dp', 'emb')), may hold values from -6 to 6
Outputs:
- output: bfloat16 [32768, 768], P(('dp', 'emb'))
- grad_pixels: float32 [32768, 768], P(('dp', 'emb'))
- grad_table: float32 [33024, 768], P('emb', 'dp')
- grad_pos_table: float32 [256, 768], P(('dp', 'emb'))
- grad_w_patch: float32 [768, 768], P(('dp', 'emb'))
- grad_w_res_a: float32 [768, 768], P(('dp', 'emb'))
- grad_w_res_b: float32 [768, 768], P(('dp', 'emb'))
- grad_gain_one: float32 [768], P(('dp', 'emb'))
- grad_bias_one: float32 [768], P(('dp', 'emb'))
- grad_w_q: float32 [768, 768], P(('dp', 'emb'))
- grad_w_k: float32 [768, 768], P(('dp', 'emb'))
- grad_w_v: float32 [768, 768], P(('dp', 'emb'))
- grad_w_o: float32 [768, 768], P(('dp', 'emb'))
- grad_gain_two: float32 [768], P(('dp', 'emb'))
- grad_bias_two: float32 [768], P(('dp', 'emb'))
- grad_w_up: float32 [768, 3072], P(('dp', 'emb'))
- grad_w_down: float32 [3072, 768], P(('dp', 'emb'))
Inputs may be any that keep to these rules, and one draw needn't show every extreme that they name: Sequence s opens with counts[s, 0] image patches and closes with counts[s, 1] actions, 1 to 192 of them; text fills the rest. Some sequence has no patches, some has 511, some has 192 actions. `token_ids`: text ids are under 32000. Of one sequence's text and action tokens (an action's row is 32000 + its bin), at most 192 have rows in one aligned block of 4128 table rows, and in each sequence some block has exactly 192.
All inputs are finite; a program needn't handle non-finite values.
Results may differ from a plain program's by a relative error of at most 0.02.
Values may be sent and summed in bfloat16 or wider, within the bound.
A program may use at most 576 MiB of HBM per device.

v0:
```python
import functools

import jax
import jax.numpy as jnp
from jax import lax
from jax.experimental import pallas as pl
from jax.experimental.pallas import tpu as pltpu
from jax.sharding import PartitionSpec as P

HEAD_DIM = 32
TEXT_VOCAB = 32000
BLOCK = 256
HEADS_STEP = 2
MESH = pl.DeviceIdType.MESH
LOG2_E = 1.4426950408889634


def normalize(values):
    average = jnp.mean(values, -1, keepdims=True)
    centred = values - average
    variance = jnp.mean(centred * centred, -1, keepdims=True)
    return centred * lax.rsqrt(variance + 1e-05)


def norm_affine(values, gain, offset):
    return normalize(values) * gain + offset


def contract(left, right, left_dim, right_dim):
    return lax.dot_general(
        left, right, (((left_dim,), (right_dim,)), ((), ())), preferred_element_type=jnp.float32
    )


def product(left, right):
    return contract(left, right, 1, 0)


def product_left(left, right):
    return contract(left, right, 0, 0)


def product_right(left, right):
    return contract(left, right, 1, 1)


def forward_kernel(heads, q_ref, k_ref, v_ref, o_ref, p_ref, r_ref):
    length = q_ref.shape[1]
    scaling = HEAD_DIM ** (-0.5) * LOG2_E
    key_place = lax.broadcasted_iota(jnp.int32, (BLOCK, BLOCK), 0)
    query_place = lax.broadcasted_iota(jnp.int32, (BLOCK, BLOCK), 1)
    allowed = key_place <= query_place
    for head in range(heads):
        rows = slice(head * HEAD_DIM, (head + 1) * HEAD_DIM)
        keys = k_ref[rows, :]
        values = v_ref[rows, :]
        for step in range(length // BLOCK):
            start, end = step * BLOCK, (step + 1) * BLOCK
            scores = contract(keys[:, :end], q_ref[rows, start:end], 0, 0) * scaling
            corner = jnp.where(allowed, scores[start:], -1e30)
            highest = jnp.max(corner, 0, keepdims=True)
            if step:
                highest = jnp.maximum(highest, jnp.max(scores[:start], 0, keepdims=True))
            weights = jnp.exp2(corner - highest)
            total = jnp.sum(weights, 0, keepdims=True)
            weights = weights.astype(jnp.bfloat16)
            if step:
                above = jnp.exp2(scores[:start] - highest)
                total = total + jnp.sum(above, 0, keepdims=True)
                weights = jnp.concatenate([above.astype(jnp.bfloat16), weights], 0)
            inverse = 1.0 / total
            base = BLOCK * (step * (step + 1) // 2)
            p_ref[head, base : base + end, :] = weights
            r_ref[head, :, start:end] = inverse
            o_ref[rows, start:end] = (
                contract(values[:, :end], weights, 1, 0) * inverse
            ).astype(jnp.bfloat16)


def packed_rows(length):
    steps = length // BLOCK
    return BLOCK * (steps * (steps + 1) // 2)


def attention_forward(queries, key_heads, values):
    width, length = queries.shape
    heads = width // HEAD_DIM
    packed = packed_rows(length)
    rows = pl.BlockSpec((HEADS_STEP * HEAD_DIM, length), lambda g: (g, 0))
    return pl.pallas_call(
        functools.partial(forward_kernel, HEADS_STEP),
        grid=(heads // HEADS_STEP,),
        in_specs=[rows] * 3,
        out_specs=[
            rows,
            pl.BlockSpec((HEADS_STEP, packed, BLOCK), lambda g: (g, 0, 0)),
            pl.BlockSpec((HEADS_STEP, 1, length), lambda g: (g, 0, 0)),
        ],
        out_shape=[
            jax.ShapeDtypeStruct((width, length), jnp.bfloat16),
            jax.ShapeDtypeStruct((heads, packed, BLOCK), jnp.bfloat16),
            jax.ShapeDtypeStruct((heads, 1, length), jnp.float32),
        ],
        compiler_params=pltpu.CompilerParams(vmem_limit_bytes=32 << 20),
        cost_estimate=pl.CostEstimate(
            flops=50_000_000_000, bytes_accessed=heads * packed * BLOCK * 2, transcendentals=0
        ),
        name="attention_forward",
    )(queries, key_heads, values)


def backward_kernel(
    heads,
    q_ref,
    k_ref,
    v_ref,
    o_ref,
    g_ref,
    p_ref,
    r_ref,
    pack_one,
    pack_two,
    part_ref,
    d_ref,
    out_one,
    out_two,
    ring_ref,
    s_ref,
    *refs,
):
    ring = Ring(part_ref, ring_ref, refs[:3])
    first, second = shares_of([pack_one, pack_two], [out_one, out_two], refs[3:])
    bits = first.bits
    number = pl.program_id(0)
    last = pl.num_programs(0) - 1

    @pl.when(number == 0)
    def begin():
        greet(False)
        first.start()
        second.start()
        ring.start()

    @pl.when(number == 1)
    def first_swap():
        first.take(0)

    @pl.when(number == 4)
    def next_swap():
        first.take(1)
        second.take(0)

    @pl.when(number == 7)
    def other_swaps():
        for stage in range(2, bits):
            first.take(stage)

    @pl.when(number == 8)
    def late_swap():
        second.take(1)

    @pl.when(number == 10)
    def last_swaps():
        for stage in range(2, bits):
            second.take(stage)

    length = q_ref.shape[1]
    steps = length // BLOCK
    scaling = HEAD_DIM ** (-0.5)
    for head in range(heads):
        rows = slice(head * HEAD_DIM, (head + 1) * HEAD_DIM)
        grads = (g_ref[rows, :].astype(jnp.float32) * r_ref[head]).astype(jnp.bfloat16)
        inner = jnp.sum(
            grads.astype(jnp.float32) * o_ref[rows, :].astype(jnp.float32), 0, keepdims=True
        )
        queries = q_ref[rows, :]
        keys = k_ref[rows, :]
        values = v_ref[rows, :]
        for step in range(steps):
            start, end = step * BLOCK, (step + 1) * BLOCK
            base = BLOCK * (step * (step + 1) // 2)
            grad_probs = contract(values[:, :end], grads[:, start:end], 0, 0)
            grad_scores = p_ref[head, base : base + end, :] * (
                grad_probs - inner[:, start:end]
            ).astype(jnp.bfloat16)
            s_ref[head, base : base + end, :] = grad_scores
            d_ref[0, rows, start:end] = (
                contract(keys[:, :end], grad_scores, 1, 0) * scaling
            ).astype(jnp.bfloat16)
        for column in range(steps):
            grad_keys = jnp.zeros((HEAD_DIM, BLOCK), jnp.float32)
            grad_values = jnp.zeros((HEAD_DIM, BLOCK), jnp.float32)
            for step in range(column, steps):
                base = BLOCK * (step * (step + 1) // 2 + column)
                span = slice(step * BLOCK, (step + 1) * BLOCK)
                grad_values = grad_values + contract(
                    grads[:, span], p_ref[head, base : base + BLOCK, :], 1, 1
                )
                grad_keys = grad_keys + contract(
                    queries[:, span], s_ref[head, base : base + BLOCK, :], 1, 1
                )
            span = slice(column * BLOCK, (column + 1) * BLOCK)
            d_ref[1, rows, span] = (grad_keys * scaling).astype(jnp.bfloat16)
            d_ref[2, rows, span] = grad_values.astype(jnp.bfloat16)

    @pl.when(number == last)
    def end():
        ring.finish()
        first.finish()
        second.finish()


def attention_backward(
    queries, key_heads, values, attended, grads, probs, inverse, packs, part
):
    width, length = queries.shape
    heads = width // HEAD_DIM
    packed = packed_rows(length)
    rows = pl.BlockSpec((HEADS_STEP * HEAD_DIM, length), lambda g: (g, 0))
    scratch = [pltpu.VMEM((HEADS_STEP, packed, BLOCK), jnp.bfloat16)]
    scratch = scratch + ring_scratch(part.shape)
    for pack in packs:
        scratch = scratch + shares_scratch(pack.shape)
    return pl.pallas_call(
        functools.partial(backward_kernel, HEADS_STEP),
        grid=(heads // HEADS_STEP,),
        in_specs=[rows] * 5
        + [
            pl.BlockSpec((HEADS_STEP, packed, BLOCK), lambda g: (g, 0, 0)),
            pl.BlockSpec((HEADS_STEP, 1, length), lambda g: (g, 0, 0)),
            pl.BlockSpec(memory_space=pl.ANY),
            pl.BlockSpec(memory_space=pl.ANY),
            pl.BlockSpec(part.shape, lambda g: (0, 0, 0)),
        ],
        out_specs=[
            pl.BlockSpec((3, HEADS_STEP * HEAD_DIM, length), lambda g: (0, g, 0)),
            pl.BlockSpec(packs[0].shape[-2:], lambda g: (0, 0)),
            pl.BlockSpec(packs[1].shape[-2:], lambda g: (0, 0)),
            pl.BlockSpec(part.shape[-2:], lambda g: (0, 0)),
        ],
        out_shape=[
            jax.ShapeDtypeStruct((3, width, length), jnp.bfloat16),
            jax.ShapeDtypeStruct(packs[0].shape[-2:], jnp.float32),
            jax.ShapeDtypeStruct(packs[1].shape[-2:], jnp.float32),
            jax.ShapeDtypeStruct(part.shape[-2:], jnp.float32),
        ],
        scratch_shapes=scratch,
        compiler_params=pltpu.CompilerParams(
            collective_id=2, has_side_effects=True, vmem_limit_bytes=56 << 20
        ),
        name="attention_backward",
    )(queries, key_heads, values, attended, grads, probs, inverse, *packs, part)


def bit_of(index, bit):
    return lax.rem(lax.div(index, 1 << bit), 2)


def flipped(index, bit):
    return index + (1 - 2 * bit_of(index, bit)) * (1 << bit)


def spans_of(rows):
    first = (rows + 31) // 32 * 16
    return ((0, first), (first, rows - first))


class Shares:
    def __init__(self, pack, out, refs):
        self.pack, self.out = pack, out
        self.groups = pack.shape[0]
        self.bits = len(pack.shape) - 3
        self.spans = spans_of(pack.shape[-2])
        refs = list(refs)
        self.own, self.zero = refs[:2]
        count = self.bits - 1
        self.later = [refs[2 + half * count : 2 + (half + 1) * count] for half in range(2)]
        refs = refs[2 + 2 * count :]
        self.ring = refs[:2]
        self.local_sem, self.swap_send, self.swap_got, self.ring_send, self.ring_got = refs[2:]
        self.emb = lax.axis_index("emb")
        self.group = lax.axis_index("dp")
        self.every = (slice(None),) * self.bits

    def order(self, half):
        rest = list(range(1, self.bits))
        return [0] + (rest if half == 0 else rest[::-1])

    def span(self, half):
        return pl.ds(*self.spans[half])

    def place(self, half, stage, mine):
        order = self.order(half)
        index = []
        for bit in range(self.bits - 1, 0, -1):
            value = bit_of(self.emb, bit)
            if order.index(bit) < stage:
                index.append(value)
            elif order.index(bit) == stage:
                index.append(value if mine else 1 - value)
            else:
                index.append(slice(None))
        return tuple(index)

    def swap(self, half, stage):
        if stage == 0:
            other = 1 - bit_of(self.emb, 0)
            source = self.pack.at[self.every + (other, self.span(half))]
            target = self.zero.at[self.every + (self.span(half),)]
        else:
            place = self.place(half, stage, False)
            source = self.own.at[(slice(None),) + place + (self.span(half),)]
            target = self.later[half][stage - 1]
        return pltpu.make_async_remote_copy(
            src_ref=source,
            dst_ref=target,
            send_sem=self.swap_send.at[half, stage],
            recv_sem=self.swap_got.at[half, stage],
            device_id={"emb": flipped(self.emb, self.order(half)[stage])},
            device_id_type=MESH,
        )

    def bring(self, half):
        mine = bit_of(self.emb, 0)
        return pltpu.make_async_copy(
            self.pack.at[self.every + (mine, self.span(half))],
            self.own.at[self.every + (self.span(half),)],
            self.local_sem.at[half],
        )

    def hop(self, half, step):
        other = lax.rem(self.group + step, self.groups)
        place = (other,) + self.place(half, self.bits, True) + (self.span(half),)
        return pltpu.make_async_remote_copy(
            src_ref=self.own.at[place],
            dst_ref=self.ring[half].at[step - 1],
            send_sem=self.ring_send.at[half, step - 1],
            recv_sem=self.ring_got.at[half, step - 1],
            device_id={"dp": other},
            device_id_type=MESH,
        )

    def start(self):
        for half in range(2):
            self.swap(half, 0).start()
            self.bring(half).start()

    def take(self, stage):
        for half in range(2):
            self.take_half(half, stage)

    def take_half(self, half, stage):
        if stage == 0:
            self.bring(half).wait()
        self.swap(half, stage).wait()
        place = self.place(half, stage, True)
        free = [n for n, index in enumerate(place) if isinstance(index, slice)]

        def one(number, carry):
            group = lax.rem(number, self.groups)
            rest = lax.div(number, self.groups)
            index = list(place)
            there = []
            for n in free:
                index[n] = lax.rem(rest, 2)
                there.append(index[n])
                rest = lax.div(rest, 2)
            target = (group,) + tuple(index) + (self.span(half), slice(None))
            if stage == 0:
                arrived = self.zero[target]
            else:
                arrived = self.later[half][stage - 1][(group,) + tuple(there)]
            total = self.own[target].astype(jnp.float32) + arrived.astype(jnp.float32)
            self.own[target] = total.astype(jnp.bfloat16)
            return carry

        lax.fori_loop(0, self.groups * 2 ** len(free), one, 0)
        if stage + 1 < self.bits:
            self.swap(half, stage + 1).start()
        elif self.out is not None:
            for step in range(1, self.groups):
                self.hop(half, step).start()

    def export(self, target):
        for half in range(2):
            place = (slice(None),) + self.place(half, self.bits, True)
            target[:, self.span(half), :] = self.own[place + (self.span(half), slice(None))]

    def finish(self):
        for half in range(2):
            place = (self.group,) + self.place(half, self.bits, True)
            total = self.own[place + (self.span(half), slice(None))].astype(jnp.float32)
            for step in range(1, self.groups):
                self.hop(half, step).wait()
                total = total + self.ring[half][step - 1].astype(jnp.float32)
            self.out[self.span(half), :] = total


class Ring:
    def __init__(self, own, out, refs):
        self.own, self.out = own, out
        self.landed, self.send, self.got = refs
        self.groups = own.shape[0]
        self.group = lax.axis_index("dp")

    def hop(self, step):
        other = lax.rem(self.group + step, self.groups)
        return pltpu.make_async_remote_copy(
            src_ref=self.own.at[other],
            dst_ref=self.landed.at[step - 1],
            send_sem=self.send.at[step - 1],
            recv_sem=self.got.at[step - 1],
            device_id={"dp": other},
            device_id_type=MESH,
        )

    def start(self):
        for step in range(1, self.groups):
            self.hop(step).start()

    def finish(self):
        total = self.own[self.group].astype(jnp.float32)
        for step in range(1, self.groups):
            self.hop(step).wait()
            total = total + self.landed[step - 1].astype(jnp.float32)
        self.out[...] = total


def ring_scratch(shape):
    groups = shape[0]
    semaphores = pltpu.SemaphoreType.DMA((groups - 1,))
    return [pltpu.VMEM((groups - 1,) + shape[1:], jnp.bfloat16), semaphores, semaphores]


def shares_scratch(shape):
    groups, bits, columns = shape[0], len(shape) - 3, shape[-1]
    whole = pltpu.VMEM((groups,) + (2,) * (bits - 1) + shape[-2:], jnp.bfloat16)
    later = [
        pltpu.VMEM((groups,) + (2,) * (bits - 1 - stage) + (span[1], columns), jnp.bfloat16)
        for span in spans_of(shape[-2])
        for stage in range(1, bits)
    ]
    ring = [
        pltpu.VMEM((groups - 1, span[1], columns), jnp.bfloat16) for span in spans_of(shape[-2])
    ]
    semaphores = [(2,), (2, bits), (2, bits), (2, groups - 1), (2, groups - 1)]
    return [whole, whole, *later, *ring] + [pltpu.SemaphoreType.DMA(size) for size in semaphores]


def shares_of(packs, outs, refs):
    bits = len(packs[0].shape) - 3
    each = 2 + 2 * (bits - 1) + 2 + 5
    return [
        Shares(pack, out, refs[n * each : (n + 1) * each])
        for n, (pack, out) in enumerate(zip(packs, outs))
    ]


def greet(everyone, ring=True):
    emb, group = lax.axis_index("emb"), lax.axis_index("dp")
    owners, groups = lax.axis_size("emb"), lax.axis_size("dp")
    barrier = pltpu.get_barrier_semaphore()
    if everyone:
        others = [lax.rem(emb + step, owners) for step in range(1, owners)]
    else:
        others = [flipped(emb, bit) for bit in range(owners.bit_length() - 1)]
    for other in others:
        pl.semaphore_signal(barrier, inc=1, device_id={"emb": other}, device_id_type=MESH)
    for step in range(1, groups if ring else 1):
        other = lax.rem(group + step, groups)
        pl.semaphore_signal(barrier, inc=1, device_id={"dp": other}, device_id_type=MESH)
    pl.semaphore_wait(barrier, len(others) + (groups - 1 if ring else 0))


def blocks_of(array):
    owners, groups = lax.axis_size("emb"), lax.axis_size("dp")
    bits = owners.bit_length() - 1
    return array.reshape((groups,) + (2,) * bits + array.shape[1:])


def rows_of(array):
    devices = lax.axis_size("emb") * lax.axis_size("dp")
    return array.astype(jnp.bfloat16).reshape(devices, array.shape[0] // devices, array.shape[1])


def stacked(pieces):
    rows = sum(piece.shape[1] for piece in pieces)
    devices, _, columns = pieces[0].shape
    spare = -rows % 16
    if rows + spare < 32:
        spare = 32 - rows
    if spare:
        pieces = pieces + [jnp.zeros((devices, spare, columns), jnp.bfloat16)]
    return blocks_of(jnp.concatenate(pieces, 1))


def vector_rows(vectors):
    devices = lax.axis_size("emb") * lax.axis_size("dp")
    return jnp.broadcast_to(vectors.astype(jnp.bfloat16)[None], (devices,) + vectors.shape)


def table_scratch(groups, owners, columns, length, capacity):
    wide = groups * capacity
    return [
        pltpu.VMEM((groups, columns, length), jnp.bfloat16),
        pltpu.VMEM((owners, columns, wide), jnp.bfloat16),
        pltpu.VMEM((owners - 1, columns, wide), jnp.bfloat16),
        pltpu.SemaphoreType.DMA((1,)),
        pltpu.SemaphoreType.DMA((groups - 1,)),
        pltpu.SemaphoreType.DMA((groups - 1,)),
        pltpu.SemaphoreType.DMA((owners - 1,)),
        pltpu.SemaphoreType.DMA((owners - 1,)),
    ]


class Table:
    def __init__(self, grads, slots, ids, out, refs):
        self.grads, self.slots, self.ids, self.out = grads, slots, ids, out
        self.turned, self.packed, self.landed = refs[:3]
        self.local_sem, self.ring_send, self.ring_got, self.send, self.got = refs[3:]
        self.groups, self.columns, self.length = self.turned.shape
        self.owners, _, self.wide = self.packed.shape
        self.capacity = self.wide // self.groups
        self.emb = lax.axis_index("emb")
        self.group = lax.axis_index("dp")

    def bring(self):
        return pltpu.make_async_copy(
            self.grads.at[self.group], self.turned.at[0], self.local_sem.at[0]
        )

    def hop(self, step):
        other = lax.rem(self.group + step, self.groups)
        return pltpu.make_async_remote_copy(
            src_ref=self.grads.at[other],
            dst_ref=self.turned.at[step],
            send_sem=self.ring_send.at[step - 1],
            recv_sem=self.ring_got.at[step - 1],
            device_id={"dp": other},
            device_id_type=MESH,
        )

    def give(self, step):
        other = lax.rem(self.emb + step, self.owners)
        return pltpu.make_async_remote_copy(
            src_ref=self.packed.at[other],
            dst_ref=self.landed.at[step - 1],
            send_sem=self.send.at[step - 1],
            recv_sem=self.got.at[step - 1],
            device_id={"emb": other},
            device_id_type=MESH,
        )

    def start(self):
        self.bring().start()
        for step in range(1, self.groups):
            self.hop(step).start()

    def arrive(self):
        self.bring().wait()
        for step in range(1, self.groups):
            self.hop(step).wait()

    def sort(self, step):
        owner = lax.rem(self.emb + step, self.owners)
        rows = lax.broadcasted_iota(jnp.int32, (128, self.length), 0)
        tiles = []
        for tile in range(self.wide // 128):
            total = jnp.zeros((self.columns, 128), jnp.float32)
            for group in range(self.groups):
                low, high = group * self.capacity, (group + 1) * self.capacity
                if high <= tile * 128 or low >= (tile + 1) * 128:
                    continue
                slot = rows + (tile * 128 - low)
                inside = (slot >= 0) & (slot < self.capacity)
                wanted = jnp.where(inside, slot + owner * self.capacity, -2)
                hot = jnp.where(wanted == self.slots[group], 1.0, 0.0).astype(jnp.bfloat16)
                total = total + product_right(self.turned[group], hot)
            tiles.append(total.astype(jnp.bfloat16))
        self.packed[owner] = jnp.concatenate(tiles, 1)
        return owner

    def add(self, step, first):
        source = lax.rem(self.emb - step + self.owners, self.owners)
        rows, columns = self.out.shape
        count = 6 if rows % 48 == 0 else 1
        block = rows // count
        chunk = self.packed[self.emb] if step == 0 else self.landed[step - 1]

        def one(number, carry):
            base = pl.multiple_of(number * block, 8)
            places = base + lax.broadcasted_iota(jnp.int32, (block, self.wide), 0)
            hot = jnp.where(places == self.ids[source], 1.0, 0.0).astype(jnp.bfloat16)
            part = product_right(hot, chunk)
            if not first:
                part = part + self.out[pl.ds(base, block), :]
            self.out[pl.ds(base, block), :] = part
            return carry

        lax.fori_loop(0, count, one, 0)


class Residual:
    def __init__(self, counts, grads, place, sources, weights, out, refs):
        self.counts, self.grads, self.place, self.out = counts, grads, place, out
        self.pixels, self.first, self.act, self.slope = sources
        self.w_a, self.w_b = weights
        self.mixed, self.inner, self.spots, self.pack = refs

    def rows_back(self):
        length, width = self.grads.shape
        block = min(512, length)

        def one(number, carry):
            base = pl.multiple_of(number * block, block)
            rows = pl.ds(base, block)
            token = base + lax.broadcasted_iota(jnp.int32, (block, width), 0)
            image = jnp.where(token < self.counts[0, 0], self.grads[rows, :], 0.0)
            mixed = image.astype(jnp.bfloat16)
            self.mixed[rows, :] = mixed
            inner = product_right(mixed, self.w_b[...]) * self.slope[rows, :].astype(jnp.float32)
            inner = inner.astype(jnp.bfloat16)
            self.inner[rows, :] = inner
            self.out[rows, :] = (image + product_right(inner, self.w_a[...])).astype(jnp.bfloat16)
            return carry

        lax.fori_loop(0, length // block, one, 0)

    def weights(self):
        length, width = self.grads.shape
        groups, bits = self.pack.shape[0], len(self.pack.shape) - 3
        devices = groups << bits
        share = width // devices
        places = self.spots.shape[0]
        spot = lax.broadcasted_iota(jnp.int32, (places, length), 0)
        hot = jnp.where(spot == self.place[...], 1.0, 0.0).astype(jnp.bfloat16)
        self.spots[...] = product(hot, self.mixed[...])
        spare = self.pack.shape[-2] - 3 * share - places // devices
        part = 384
        for start in range(0, width, part):
            span = slice(start, start + part)
            pieces = [
                product_left(self.pixels[:, span], self.out[...]),
                product_left(self.first[:, span], self.inner[...]),
                product_left(self.act[:, span], self.mixed[...]),
            ]
            for place in range(part // share):
                device = start // share + place
                rows = [piece[place * share : (place + 1) * share] for piece in pieces]
                each = places // devices
                rows.append(self.spots[device * each : (device + 1) * each, :])
                if spare:
                    rows.append(jnp.zeros((spare, width), jnp.float32))
                owner = device % (1 << bits)
                index = tuple((owner >> bit) & 1 for bit in range(bits - 1, -1, -1))
                self.pack[(device >> bits,) + index] = jnp.concatenate(rows, 0).astype(
                    jnp.bfloat16
                )


def tail_kernel(inside, grads_ref, slots_ref, ids_ref, *refs):
    if inside:
        inputs, refs = refs[:10], refs[10:]
        table_out, *outs = refs[:3]
        low_ref, refs = refs[3], refs[4:]
        residual = Residual(
            inputs[1], inputs[2], inputs[3], inputs[4:8], inputs[8:10], low_ref, refs[:4]
        )
        packs = [inputs[0], residual.pack]
        refs = refs[4:]
    else:
        packs, (table_out, *outs), refs = refs[:2], refs[2:5], refs[5:]
    table = Table(grads_ref, slots_ref, ids_ref, table_out, refs[:8])
    first, second = shares_of(packs, outs, refs[8:])
    owners = table.owners
    greet(True)
    table.start()
    first.start()
    if inside:
        residual.rows_back()
        first.take(0)
        residual.weights()
        second.start()
    else:
        second.start()
        first.take(0)
    for stage in range(1, first.bits):
        first.take(stage)
        second.take(stage - 1)
    second.take(second.bits - 1)
    table.arrive()
    for step in range(1, owners):
        table.sort(step)
        table.give(step).start()
    table.sort(0)
    table.add(0, True)
    first.finish()
    second.finish()
    for step in range(1, owners):
        table.give(step).wait()
        table.add(step, False)


def tail(grads, slots, ids, pack, extra, table_rows, capacity, inside):
    groups, columns, length = grads.shape
    owners = ids.shape[0]
    anywhere = pl.BlockSpec(memory_space=pl.ANY)
    vmem = pl.BlockSpec(memory_space=pltpu.VMEM)
    smem = pl.BlockSpec(memory_space=pltpu.SMEM)
    width = pack.shape[-1]
    own = []
    outs = [jax.ShapeDtypeStruct((table_rows, columns), jnp.float32)]
    outs.append(jax.ShapeDtypeStruct(pack.shape[-2:], jnp.float32))
    if inside:
        devices = groups * owners
        rows = 3 * (width // devices) + inside // devices
        rows = max(32, rows + -rows % 16)
        shape = pack.shape[:-2] + (rows, width)
        own = [
            pltpu.VMEM((length, width), jnp.bfloat16),
            pltpu.VMEM((length, width), jnp.bfloat16),
            pltpu.VMEM((inside, width), jnp.float32),
            pltpu.VMEM(shape, jnp.bfloat16),
        ]
        specs = [anywhere, smem] + [vmem] * 8
        outs.append(jax.ShapeDtypeStruct(shape[-2:], jnp.float32))
        outs.append(jax.ShapeDtypeStruct((length, width), jnp.bfloat16))
    else:
        shape = extra[0].shape
        specs = [anywhere, anywhere]
        outs.append(jax.ShapeDtypeStruct(shape[-2:], jnp.float32))
    scratch = own + table_scratch(groups, owners, columns, length, capacity)
    scratch = scratch + shares_scratch(pack.shape) + shares_scratch(shape)
    return pl.pallas_call(
        functools.partial(tail_kernel, inside),
        in_specs=[anywhere, vmem, vmem] + specs,
        out_specs=[vmem] * len(outs),
        out_shape=outs,
        scratch_shapes=scratch,
        compiler_params=pltpu.CompilerParams(
            collective_id=3, has_side_effects=True, vmem_limit_bytes=60 << 20
        ),
        name="tail",
    )(grads, slots, ids, pack, *extra)


def column_of(row, rows):
    diagonal = lax.broadcasted_iota(jnp.int32, (128, 128), 0) == lax.broadcasted_iota(
        jnp.int32, (128, 128), 1
    )
    pieces = [
        jnp.sum(jnp.where(diagonal, row[:, start : start + 128], 0), 1, keepdims=True)
        for start in range(0, rows, 128)
    ]
    return jnp.concatenate(pieces, 0)


def gelu_pair(value):
    root = 0.7978845608028654
    square = value * value
    bend = jnp.tanh(root * (value + 0.044715 * (value * square)))
    half = 0.5 * (1.0 + bend)
    slope = half + 0.5 * value * (1.0 - bend * bend) * (root * (1.0 + 3 * 0.044715 * square))
    return value * half, slope


def front_kernel(
    counts_ref,
    codes_ref,
    place_ref,
    pixels_ref,
    table_ref,
    pos_ref,
    w_patch_ref,
    w_a_ref,
    w_b_ref,
    gain_ref,
    bias_ref,
    embedded_ref,
    normed_ref,
    first_ref,
    act_ref,
    slope_ref,
    ids_ref,
    slots_ref,
    codes_all,
    ranks,
    earlier,
    held,
    packed,
    landed,
    fetched,
    mixed,
    local_sem,
    ask_send,
    ask_got,
    send,
    got,
):
    owners, capacity, width = packed.shape
    length = codes_ref.shape[1]
    table_rows = held.shape[0]
    emb = lax.axis_index("emb")
    bring = pltpu.make_async_copy(table_ref, held, local_sem.at[0])
    bring.start()
    barrier = pltpu.get_barrier_semaphore()
    for step in range(1, owners):
        other = lax.rem(emb + step, owners)
        pl.semaphore_signal(barrier, inc=1, device_id={"emb": other}, device_id_type=MESH)
    pl.semaphore_wait(barrier, owners - 1)

    def ask(step):
        return pltpu.make_async_remote_copy(
            src_ref=codes_ref,
            dst_ref=codes_all.at[step],
            send_sem=ask_send.at[step - 1],
            recv_sem=ask_got.at[step - 1],
            device_id={"emb": lax.rem(emb + step, owners)},
            device_id_type=MESH,
        )

    def give(step):
        return pltpu.make_async_remote_copy(
            src_ref=packed.at[step],
            dst_ref=landed.at[step - 1],
            send_sem=send.at[step - 1],
            recv_sem=got.at[step - 1],
            device_id={"emb": lax.rem(emb - step + owners, owners)},
            device_id_type=MESH,
        )

    for step in range(1, owners):
        ask(step).start()
    codes_all[0] = codes_ref[...]
    block = min(256, length)

    def triangle(number, carry):
        base = pl.multiple_of(number * block, block)
        above = base + lax.broadcasted_iota(jnp.int32, (block, length), 0)
        below = lax.broadcasted_iota(jnp.int32, (block, length), 1)
        earlier[pl.ds(base, block), :] = jnp.where(above < below, 1.0, 0.0).astype(jnp.bfloat16)
        return carry

    lax.fori_loop(0, length // block, triangle, 0)
    codes = codes_ref[...]
    mine = [
        (codes >= owner * table_rows) & (codes < (owner + 1) * table_rows)
        for owner in range(owners)
    ]
    marks = jnp.concatenate([jnp.where(mark, 1.0, 0.0) for mark in mine], 0)
    places = product(marks.astype(jnp.bfloat16), earlier[...])
    slots = jnp.full((1, length), owners * capacity, jnp.int32)
    for owner in range(owners):
        rank = places[owner : owner + 1].astype(jnp.int32)
        slots = jnp.where(mine[owner], owner * capacity + rank, slots)
    slots_ref[...] = slots
    for step in range(1, owners):
        ask(step).wait()
    local = codes_all[...].reshape(owners, length) - emb * table_rows
    inside = (local >= 0) & (local < table_rows)
    places = product(jnp.where(inside, 1.0, 0.0).astype(jnp.bfloat16), earlier[...])
    ranks[...] = jnp.where(inside, places.astype(jnp.int32), -1).reshape(owners, 1, length)
    bring.wait()

    def gather(step):
        rank = ranks[step]
        local = codes_all[step] - emb * table_rows + 1
        slot = lax.broadcasted_iota(jnp.int32, (capacity, length), 0)
        match = slot == rank
        hot = jnp.where(match, 1.0, 0.0).astype(jnp.bfloat16)
        coarse = lax.div(local, 64)
        fine = local - coarse * 64
        inner = rank >= 0
        pair = jnp.concatenate(
            [jnp.where(inner, coarse, 0), jnp.where(inner, fine, 0)]
            + [jnp.zeros((6, length), jnp.int32)],
            0,
        )
        pair = product_right(pair.astype(jnp.float32).astype(jnp.bfloat16), hot)
        source = lax.rem(emb - step + owners, owners)
        ids_ref[source] = (pair[0:1] * 64.0 + pair[1:2]).astype(jnp.int32) - 1
        wanted = jnp.sum(jnp.where(match, local, 0), 1, keepdims=True) - 1
        total = jnp.zeros((capacity, width), jnp.float32)
        for start in range(0, table_rows, 1024):
            size = min(1024, table_rows - start)
            row = start + lax.broadcasted_iota(jnp.int32, (capacity, size), 1)
            hot = jnp.where(row == wanted, 1.0, 0.0).astype(jnp.bfloat16)
            total = total + product(hot, held[start : start + size, :])
        packed[step] = total.astype(jnp.bfloat16)

    def serve(step, carry):
        gather(step)
        give(step).start()
        return carry

    lax.fori_loop(1, owners, serve, 0)
    gather(0)
    slot_column = column_of(slots, length)
    fetched[...] = jnp.zeros_like(fetched)

    def place_rows(step):
        owner = lax.rem(emb + step, owners)
        rows = packed[0] if step == 0 else landed[step - 1]
        for start in range(0, length, block):
            slot = owner * capacity + lax.broadcasted_iota(jnp.int32, (block, capacity), 1)
            hot = jnp.where(slot == slot_column[start : start + block], 1.0, 0.0)
            fetched[start : start + block, :] += product(hot.astype(jnp.bfloat16), rows)


    def patches(number, carry):
        base = pl.multiple_of(number * block, block)
        rows = pl.ds(base, block)
        first = product(pixels_ref[rows, :], w_patch_ref[...])
        low = first.astype(jnp.bfloat16)
        first_ref[rows, :] = low
        act, slope = gelu_pair(product(low, w_a_ref[...]))
        act = act.astype(jnp.bfloat16)
        act_ref[rows, :] = act
        slope_ref[rows, :] = slope.astype(jnp.bfloat16)
        mixed[rows, :] = first + product(act, w_b_ref[...])
        return carry

    lax.fori_loop(0, length // block, patches, 0)

    def positions(number, carry):
        base = pl.multiple_of(number * block, block)
        spot = lax.broadcasted_iota(jnp.int32, (block, pos_ref.shape[0]), 1)
        place = column_of(place_ref[:, pl.ds(base, block)], block)
        hot = jnp.where(spot == place, 1.0, 0.0).astype(jnp.bfloat16)
        embedded_ref[pl.ds(base, block), :] = product(hot, pos_ref[...])
        return carry

    lax.fori_loop(0, length // block, positions, 0)
    place_rows(0)
    for step in range(1, owners):
        give(step).wait()
        place_rows(step)

    def settle(number, carry):
        base = pl.multiple_of(number * block, block)
        rows = pl.ds(base, block)
        token = base + lax.broadcasted_iota(jnp.int32, (block, width), 0)
        image = mixed[rows, :] + embedded_ref[rows, :]
        value = jnp.where(token < counts_ref[0, 0], image, fetched[rows, :])
        embedded_ref[rows, :] = value
        normed = normalize(value) * gain_ref[...] + bias_ref[...]
        normed_ref[rows, :] = normed.astype(jnp.bfloat16)
        return carry

    lax.fori_loop(0, length // block, settle, 0)


def front(counts, codes, place, pixels, table, pos, w_patch, w_a, w_b, gain, bias, capacity):
    owners = lax.axis_size("emb")
    length, width = pixels.shape
    vmem = pl.BlockSpec(memory_space=pltpu.VMEM)
    low = jax.ShapeDtypeStruct((length, width), jnp.bfloat16)
    full = jax.ShapeDtypeStruct((length, width), jnp.float32)
    return pl.pallas_call(
        front_kernel,
        in_specs=[pl.BlockSpec(memory_space=pltpu.SMEM), vmem, vmem, vmem]
        + [pl.BlockSpec(memory_space=pl.ANY)]
        + [vmem] * 6,
        out_specs=[vmem] * 7,
        out_shape=[
            full,
            low,
            low,
            low,
            low,
            jax.ShapeDtypeStruct((owners, 1, capacity), jnp.int32),
            jax.ShapeDtypeStruct((1, length), jnp.int32),
        ],
        scratch_shapes=[
            pltpu.VMEM((owners, 1, length), jnp.int32),
            pltpu.VMEM((owners, 1, length), jnp.int32),
            pltpu.VMEM((length, length), jnp.bfloat16),
            pltpu.VMEM(table.shape, jnp.bfloat16),
            pltpu.VMEM((owners, capacity, width), jnp.bfloat16),
            pltpu.VMEM((owners - 1, capacity, width), jnp.bfloat16),
            pltpu.VMEM((length, width), jnp.float32),
            pltpu.VMEM((length, width), jnp.float32),
            pltpu.SemaphoreType.DMA((1,)),
            pltpu.SemaphoreType.DMA((owners - 1,)),
            pltpu.SemaphoreType.DMA((owners - 1,)),
            pltpu.SemaphoreType.DMA((owners - 1,)),
            pltpu.SemaphoreType.DMA((owners - 1,)),
        ],
        compiler_params=pltpu.CompilerParams(
            collective_id=1, has_side_effects=True, vmem_limit_bytes=56 << 20
        ),
        name="front",
    )(counts, codes, place, pixels, table, pos, w_patch, w_a, w_b, gain, bias)


def feed_kernel(
    attended_ref,
    embedded_ref,
    cotangent_ref,
    w_o_ref,
    gain_ref,
    bias_ref,
    w_up_ref,
    w_down_ref,
    output_ref,
    grad_middle_ref,
    grad_up_ref,
    grad_attended_ref,
    grad_w_o_ref,
    gains_ref,
    part_ref,
    middle,
    normed,
    back,
    slopes,
    hidden,
    pack,
    *refs,
):
    (share,) = shares_of([pack], [None], refs)
    groups, length, chunk = slopes.shape
    bits = share.bits
    owners = 1 << bits
    width = middle.shape[1]
    step = pl.program_id(0)
    block = min(512, length)
    blocks = length // block

    @pl.when(step == 0)
    def begin():
        greet(False, ring=False)

        def one(number, carry):
            rows = pl.ds(pl.multiple_of(number * block, block), block)
            value = embedded_ref[rows, :] + product_left(attended_ref[:, rows], w_o_ref[...])
            middle[rows, :] = value
            normed[rows, :] = (normalize(value) * gain_ref[...] + bias_ref[...]).astype(
                jnp.bfloat16
            )
            return carry

        lax.fori_loop(0, blocks, one, 0)

    @pl.when(step < groups)
    def go_forward():
        def one(number, carry):
            rows = pl.ds(pl.multiple_of(number * block, block), block)
            act, slope = gelu_pair(product(normed[rows, :], w_up_ref[...]))
            act = act.astype(jnp.bfloat16)
            hidden[rows, :] = act
            slopes[step, rows, :] = slope.astype(jnp.bfloat16)
            grown = product(act, w_down_ref[...])

            @pl.when(step == 0)
            def first():
                grad_middle_ref[rows, :] = middle[rows, :] + grown

            @pl.when(step > 0)
            def other():
                grad_middle_ref[rows, :] = grad_middle_ref[rows, :] + grown

            return carry

        lax.fori_loop(0, blocks, one, 0)
        units = chunk // owners
        spare = pack.shape[-2] - units
        part = 384 if chunk % 384 == 0 and 384 % units == 0 else chunk
        for start in range(0, chunk, part):
            grads = product_left(hidden[:, start : start + part], cotangent_ref[...])
            for place in range(part // units):
                piece = grads[place * units : (place + 1) * units]
                if spare:
                    piece = jnp.concatenate([piece, jnp.zeros((spare, width), jnp.float32)], 0)
                owner = start // units + place
                index = tuple((owner >> bit) & 1 for bit in range(bits - 1, -1, -1))
                pack[(step,) + index] = piece.astype(jnp.bfloat16)

    @pl.when(step == groups - 1)
    def turn():
        output_ref[...] = grad_middle_ref[...].astype(jnp.bfloat16)
        share.start()

    @pl.when(step == groups + 1)
    def swap():
        share.take(0)

    @pl.when(step >= groups)
    def go_back():
        def one(number, carry):
            rows = pl.ds(pl.multiple_of(number * block, block), block)
            slope = slopes[step - groups, rows, :].astype(jnp.float32)
            grads = product_right(cotangent_ref[rows, :], w_down_ref[...]) * slope
            grads = grads.astype(jnp.bfloat16)
            hidden[rows, :] = grads
            lower = product_right(grads, w_up_ref[...])

            @pl.when(step == groups)
            def first():
                back[rows, :] = lower

            @pl.when(step > groups)
            def other():
                back[rows, :] = back[rows, :] + lower

            return carry

        lax.fori_loop(0, blocks, one, 0)
        for start in range(0, width, 768):
            span = slice(start, start + 768)
            grad_up_ref[0, span, :] = product_left(normed[:, span], hidden[...]).astype(
                jnp.bfloat16
            )

    @pl.when(step == 2 * groups - 1)
    def end():
        share.take(1)
        gains_ref[...] = jnp.zeros_like(gains_ref)

        def one(number, carry):
            rows = pl.ds(pl.multiple_of(number * block, block), block)
            value = middle[rows, :]
            centred = value - jnp.mean(value, -1, keepdims=True)
            scale = lax.rsqrt(jnp.mean(centred * centred, -1, keepdims=True) + 1e-05)
            unit = centred * scale
            grads = back[rows, :]
            gains_ref[0:1, :] += jnp.sum(grads * unit, 0, keepdims=True)
            gains_ref[1:2, :] += jnp.sum(grads, 0, keepdims=True)
            grads = grads * gain_ref[...]
            along = jnp.mean(grads * unit, -1, keepdims=True)
            grads = scale * (grads - jnp.mean(grads, -1, keepdims=True) - unit * along)
            grads = cotangent_ref[rows, :].astype(jnp.float32) + grads
            grad_middle_ref[rows, :] = grads
            normed[rows, :] = grads.astype(jnp.bfloat16)
            return carry

        lax.fori_loop(0, blocks, one, 0)
        for start in range(0, width, 256):
            span = slice(start, start + 256)
            grad_w_o_ref[span, :] = product(attended_ref[span, :], normed[...]).astype(
                jnp.bfloat16
            )
            grad_attended_ref[span, :] = product_right(w_o_ref[span, :], normed[...]).astype(
                jnp.bfloat16
            )
        for stage in range(2, bits):
            share.take(stage)
        share.export(part_ref)


def feed(attended, embedded, cotangent, w_o, gain, bias, w_up, w_down):
    groups, owners = lax.axis_size("dp"), lax.axis_size("emb")
    length, width = embedded.shape
    chunk = w_up.shape[1] // groups
    units = chunk // owners
    units = max(32, units + -units % 16)
    shape = (groups,) + (2,) * (owners.bit_length() - 1) + (units, width)
    once = pl.Buffered(1)

    def whole(array):
        return pl.BlockSpec(array.shape, lambda s: (0, 0), pipeline_mode=once)

    outs = [
        jax.ShapeDtypeStruct((length, width), jnp.bfloat16),
        jax.ShapeDtypeStruct((length, width), jnp.float32),
        jax.ShapeDtypeStruct((groups, width, chunk), jnp.bfloat16),
        jax.ShapeDtypeStruct((width, length), jnp.bfloat16),
        jax.ShapeDtypeStruct((width, width), jnp.bfloat16),
        jax.ShapeDtypeStruct((8, width), jnp.float32),
        jax.ShapeDtypeStruct((groups, units, width), jnp.bfloat16),
    ]
    out_specs = [whole(out) if len(out.shape) == 2 else None for out in outs]
    out_specs[2] = pl.BlockSpec((1, width, chunk), lambda s: (jnp.maximum(s - groups, 0), 0, 0))
    out_specs[6] = pl.BlockSpec(outs[6].shape, lambda s: (0, 0, 0), pipeline_mode=once)
    return pl.pallas_call(
        feed_kernel,
        grid=(2 * groups,),
        in_specs=[
            whole(attended),
            whole(embedded),
            whole(cotangent),
            whole(w_o),
            whole(gain),
            whole(bias),
            pl.BlockSpec((width, chunk), lambda s: (0, lax.rem(s, groups))),
            pl.BlockSpec((chunk, width), lambda s: (lax.rem(s, groups), 0)),
        ],
        out_specs=out_specs,
        out_shape=outs,
        scratch_shapes=[
            pltpu.VMEM((length, width), jnp.float32),
            pltpu.VMEM((length, width), jnp.bfloat16),
            pltpu.VMEM((length, width), jnp.float32),
            pltpu.VMEM((groups, length, chunk), jnp.bfloat16),
            pltpu.VMEM((length, chunk), jnp.bfloat16),
            pltpu.VMEM(shape, jnp.bfloat16),
        ]
        + shares_scratch(shape),
        compiler_params=pltpu.CompilerParams(
            collective_id=4, has_side_effects=True, vmem_limit_bytes=58 << 20
        ),
        name="feed",
    )(attended, embedded, cotangent, w_o, gain, bias, w_up, w_down)


def first_kernel(
    heads_ref,
    w_q_ref,
    w_k_ref,
    w_v_ref,
    embedded_ref,
    middle_ref,
    normed_ref,
    gain_ref,
    grad_ref,
    turned_ref,
    weights_ref,
    gains_ref,
    back,
    normed_turned,
):
    length, width = embedded_ref.shape
    block = min(512, length)
    gains_ref[...] = jnp.zeros_like(gains_ref)

    def rows_back(number, carry):
        base = pl.multiple_of(number * block, block)
        rows = pl.ds(base, block)
        back[...] = product(w_q_ref[...], heads_ref[0:width, rows])
        back[...] += product(w_k_ref[...], heads_ref[width : 2 * width, rows])
        back[...] += product(w_v_ref[...], heads_ref[2 * width :, rows])
        grads = back[...].T
        value = embedded_ref[rows, :]
        centred = value - jnp.mean(value, -1, keepdims=True)
        scale = lax.rsqrt(jnp.mean(centred * centred, -1, keepdims=True) + 1e-05)
        unit = centred * scale
        gains_ref[0:1, :] += jnp.sum(grads * unit, 0, keepdims=True)
        gains_ref[1:2, :] += jnp.sum(grads, 0, keepdims=True)
        grads = grads * gain_ref[...]
        along = jnp.mean(grads * unit, -1, keepdims=True)
        grads = scale * (grads - jnp.mean(grads, -1, keepdims=True) - unit * along)
        grads = middle_ref[rows, :] + grads
        grad_ref[rows, :] = grads
        turned_ref[:, rows] = grads.T.astype(jnp.bfloat16)
        normed_turned[:, rows] = normed_ref[rows, :].astype(jnp.float32).T.astype(jnp.bfloat16)
        return carry

    lax.fori_loop(0, length // block, rows_back, 0)

    def weights(number, carry):
        base = pl.multiple_of(number * width, width)
        weights_ref[number] = product_right(
            normed_turned[...], heads_ref[pl.ds(base, width), :]
        ).astype(jnp.bfloat16)
        return carry

    lax.fori_loop(0, 3, weights, 0)


def first_backward(heads, w_q, w_k, w_v, embedded, middle, normed, gain):
    length, width = embedded.shape
    vmem = pl.BlockSpec(memory_space=pltpu.VMEM)
    return pl.pallas_call(
        first_kernel,
        in_specs=[vmem] * 8,
        out_specs=[vmem] * 4,
        out_shape=[
            jax.ShapeDtypeStruct((length, width), jnp.float32),
            jax.ShapeDtypeStruct((width, length), jnp.bfloat16),
            jax.ShapeDtypeStruct((3, width, width), jnp.bfloat16),
            jax.ShapeDtypeStruct((8, width), jnp.float32),
        ],
        scratch_shapes=[
            pltpu.VMEM((width, min(512, length)), jnp.float32),
            pltpu.VMEM((width, length), jnp.bfloat16),
        ],
        compiler_params=pltpu.CompilerParams(vmem_limit_bytes=56 << 20),
        name="first_backward",
    )(heads, w_q, w_k, w_v, embedded, middle, normed, gain)


def on_device(
    pixels,
    counts,
    token_ids,
    action_bins,
    patch_pos,
    token_table,
    pos_table,
    w_patch,
    w_res_a,
    w_res_b,
    gain_one,
    bias_one,
    w_q,
    w_k,
    w_v,
    w_o,
    gain_two,
    bias_two,
    w_up,
    w_down,
    cotangent,
):
    length = pixels.shape[0]
    model_width = w_q.shape[0]
    positions = jnp.arange(length)
    image_rows = positions < counts[0, 0]
    action_rows = positions >= length - counts[0, 1]
    table_rows = jnp.logical_not(image_rows)
    row_ids = jnp.where(action_rows, TEXT_VOCAB + action_bins, token_ids)
    rows_owned = token_table.shape[0]
    owners_total = lax.axis_size("emb")
    capacity = 3 * length // (2 * owners_total)
    groups = lax.axis_size("dp")
    codes = jnp.where(table_rows, row_ids, -1).reshape(1, length)
    gain_row = gain_one.astype(jnp.float32).reshape(1, model_width)
    bias_row = bias_one.astype(jnp.float32).reshape(1, model_width)
    embedded, normed_one, first_low, res_act, res_slope, ids, slots = front(
        counts,
        codes,
        patch_pos.reshape(1, length),
        pixels,
        token_table,
        pos_table,
        w_patch,
        w_res_a,
        w_res_b,
        gain_row,
        bias_row,
        capacity,
    )
    facts = jnp.concatenate([ids.reshape(-1), slots.reshape(-1)])
    ring = [facts] + [
        lax.ppermute(facts, "dp", [(i, (i + step) % groups) for i in range(groups)])
        for step in range(1, groups)
    ]
    ring = jnp.stack(ring)
    ring_ids = ring[:, : owners_total * capacity].reshape(groups, owners_total, capacity)
    ring_ids = jnp.swapaxes(ring_ids, 0, 1).reshape(owners_total, 1, groups * capacity)
    ring_slots = ring[:, owners_total * capacity :].reshape(groups, 1, length)
    queries = contract(w_q, normed_one, 0, 1).astype(jnp.bfloat16)
    key_heads = contract(w_k, normed_one, 0, 1).astype(jnp.bfloat16)
    value_heads = contract(w_v, normed_one, 0, 1).astype(jnp.bfloat16)
    attended, probs, inverse = attention_forward(queries, key_heads, value_heads)
    output, grad_middle, grad_w_up, grad_attended, grad_w_o, gains, part_down = feed(
        attended,
        embedded,
        cotangent,
        w_o,
        gain_two.astype(jnp.float32).reshape(1, model_width),
        bias_two.astype(jnp.float32).reshape(1, model_width),
        w_up,
        w_down,
    )
    devices = groups * owners_total
    share = model_width // devices
    folds = w_up.shape[1] // model_width
    per_fold = groups // folds
    folded = []
    for n in range(folds):
        pieces = [grad_w_up[n * per_fold + m] for m in range(per_fold)]
        folded.append(rows_of(jnp.concatenate(pieces, 1) if per_fold > 1 else pieces[0]))
    grad_heads, share_one, share_two, share_down = attention_backward(
        queries,
        key_heads,
        value_heads,
        attended,
        grad_attended,
        probs,
        inverse,
        [
            stacked(folded[:2] + [rows_of(grad_w_o), vector_rows(gains)]),
            stacked(folded[2:]),
        ],
        part_down,
    )
    grad_heads = grad_heads.reshape(3 * model_width, length)
    grad_embedded, grads_turned, grad_w_heads, gains = first_backward(
        grad_heads, w_q, w_k, w_v, embedded, grad_middle, normed_one, gain_row
    )
    gains_one = vector_rows(gains)
    grad_w_heads = [rows_of(grad_w_heads[n]) for n in range(3)]
    columns = model_width // groups
    grads_turned = grads_turned.reshape(groups, columns, length)
    pos_rows = pos_table.shape[0]
    pos_share = pos_rows // devices
    pack_heads = stacked(grad_w_heads + [gains_one])
    if share % 8 == 0 and 384 % share == 0 and pos_share % 8 == 0:
        grad_table, share_heads, share_res, grad_first = tail(
            grads_turned,
            ring_slots,
            ring_ids,
            pack_heads,
            [
                counts,
                grad_embedded,
                patch_pos.reshape(1, length),
                pixels,
                first_low,
                res_act,
                res_slope,
                w_res_a,
                w_res_b,
            ],
            rows_owned,
            capacity,
            pos_rows,
        )
    else:
        grad_image = jnp.where(image_rows[:, None], grad_embedded, 0.0)
        grad_mixed = grad_image.astype(jnp.bfloat16)
        position_hot = patch_pos[:, None] == jnp.arange(pos_rows)[None, :]
        grad_pos_table = product_left(position_hot.astype(jnp.bfloat16), grad_mixed)
        grad_w_res_b = product_left(res_act, grad_mixed)
        grad_inner = product_right(grad_mixed, w_res_b) * res_slope.astype(jnp.float32)
        grad_inner = grad_inner.astype(jnp.bfloat16)
        grad_w_res_a = product_left(first_low, grad_inner)
        grad_first = (grad_image + product_right(grad_inner, w_res_a)).astype(jnp.bfloat16)
        grad_w_patch = product_left(pixels, grad_first)
        res_rows = [rows_of(g) for g in (grad_w_patch, grad_w_res_a, grad_w_res_b, grad_pos_table)]
        grad_table, share_heads, share_res = tail(
            grads_turned,
            ring_slots,
            ring_ids,
            pack_heads,
            [stacked(res_rows)],
            rows_owned,
            capacity,
            0,
        )
    grad_pixels = product_right(grad_first, w_patch)

    def cut(array, place):
        return array[place * share : (place + 1) * share]

    rows_up = jnp.concatenate([share_one[: 2 * share], share_two[: (folds - 2) * share]], 0)
    share_w_up = jnp.swapaxes(rows_up.reshape(folds, share, model_width), 0, 1)
    place = (lax.axis_index("dp") * owners_total + lax.axis_index("emb")) * share
    gains_two = lax.dynamic_slice(share_one[3 * share : 3 * share + 2], (0, place), (2, share))
    gains_one = lax.dynamic_slice(share_heads[3 * share : 3 * share + 2], (0, place), (2, share))
    return (
        output,
        grad_pixels,
        grad_table,
        share_res[3 * share : 3 * share + pos_share],
        cut(share_res, 0),
        cut(share_res, 1),
        cut(share_res, 2),
        gains_one[0],
        gains_one[1],
        cut(share_heads, 0),
        cut(share_heads, 1),
        cut(share_heads, 2),
        cut(share_one, 2),
        gains_two[0],
        gains_two[1],
        share_w_up.reshape(share, folds * model_width),
        share_down[: w_down.shape[0] // devices],
    )


def solution(mesh):
    in_specs = (
        P(("dp", "emb"), None),
        P(("dp", "emb"), None),
        P(("dp", "emb")),
        P(("dp", "emb")),
        P(("dp", "emb")),
        P("emb", None),
        P(),
        P(),
        P(),
        P(),
        P(),
        P(),
        P(),
        P(),
        P(),
        P(),
        P(),
        P(),
        P(),
        P(),
        P(("dp", "emb"), None),
    )
    out_specs = (
        P(("dp", "emb"), None),
        P(("dp", "emb"), None),
        P("emb", "dp"),
        P(("dp", "emb"), None),
        P(("dp", "emb"), None),
        P(("dp", "emb"), None),
        P(("dp", "emb"), None),
        P(("dp", "emb")),
        P(("dp", "emb")),
        P(("dp", "emb"), None),
        P(("dp", "emb"), None),
        P(("dp", "emb"), None),
        P(("dp", "emb"), None),
        P(("dp", "emb")),
        P(("dp", "emb")),
        P(("dp", "emb"), None),
        P(("dp", "emb"), None),
    )
    return jax.shard_map(
        on_device, mesh=mesh, in_specs=in_specs, out_specs=out_specs, check_vma=False
    )
```

profile of v0, /device:TPU:1, one launch (start us, length us, event | category | flops | bytes accessed | tf_op | source)
XLA Modules:
  0.0 380.9 jit_solution(18051342928320968004)
XLA Ops:
  0.7 1.3 fusion.7
  2.0 1.3 reshape.134.gain_ref
  3.2 1.3 reshape.136.bias_ref
  5.1 1.9 select_select_fusion
  7.1 47.0 %front.1 = (f32[1024,768]{1,0:T(8,128)}, bf16[1024,768]{1,0:T(8,128)(2,1)}, bf16[1024,768]{1,0:T(8,128)(2,1)}, bf16[1024,768]{1,0:T(8,128)(2,1)}, bf16[1024,768]...) custom-call(s32[1,2]{1,0:T(1,128)} %refs_1_.1, s32[1,1024]{1,0:T(1,128)} %bitcast.58, s32[1,1024]{1,0:T(1,128)} %bitcast.59, ...), custom_call_target="tpu_custom_call" | custom-call | tf_op jit(solution)/shard_map/front/pallas_call | solution.py:959
  55.6 1.3 collective-permute-start
  56.9 2.3 collective-permute-start.1
  59.2 1.6 collective-permute-start.2
  60.8 3.0 fusion.q_ref
  63.8 1.4 fusion.1.k_ref
  65.7 1.4 fusion.2.v_ref
  68.3 45.3 %attention_forward.1 = (bf16[768,1024]{1,0:T(8,128)(2,1)S(1)}, bf16[24,2560,256]{2,1,0:T(8,128)(2,1)}, f32[24,1,1024]{2,1,0:T(1,128)S(1)}) custom-call(bf16[768,1024]{1,0:T(8,128)(2,1)S(1)} %fusion.q_ref, bf16[768,1024]{1,0:T(8,128)(2,1)S(1)} %fusion.1.k_ref, bf16[768,1024]{1,0:T(8,128)(2,1)S(1)} %fusion.2.v_ref), custom_call_target="tpu_custom_call" | custom-call | flops 49999998976 | bytes 31457280 | tf_op jit(solution)/shard_map/attention_forward/pallas_call | solution.py:90
  113.7 1.1 copy-done
  115.5 64.8 %feed.1 = (bf16[1024,768]{1,0:T(8,128)(2,1)}, f32[1024,768]{1,0:T(8,128)}, bf16[4,768,768]{2,1,0:T(8,128)(2,1)}, bf16[768,1024]{1,0:T(8,128)(2,1)}, bf16[768,768...) custom-call(bf16[768,1024]{1,0:T(8,128)(2,1)} %copy-done, ...), custom_call_target="tpu_custom_call" | custom-call | tf_op jit(solution)/shard_map/feed/pallas_call | solution.py:1174
  180.3 2.6 fusion.3
  183.0 1.6 pad_maximum_fusion.2.pack_two
  184.7 2.1 pad_maximum_fusion.pack_one
  186.8 58.3 %attention_backward.1 = (bf16[3,768,1024]{2,1,0:T(8,128)(2,1)}, f32[80,768]{1,0:T(8,128)}, f32[48,768]{1,0:T(8,128)}, f32[96,768]{1,0:T(8,128)}) custom-call(bf16[768,1024]{1,0:T(8,128)(2,1)} %copy-done.1, bf16[768,1024]{1,0:T(8,128)(2,1)} %copy-done.2, bf16[768,1024]{1,0:T(8,128)(2,1)} %copy-done.3, bf16[768,1024]{1,0:T(8,128)(2,1)} %copy-done, ...), custom_call_target="tpu_custom_call" | custom-call | tf_op jit(solution)/shard_map/attention_backward/pallas_call | solution.py:224
  245.1 0.9 slice.103
  246.0 18.2 %first_backward.1 = (f32[1024,768]{1,0:T(8,128)}, bf16[768,1024]{1,0:T(8,128)(2,1)}, bf16[3,768,768]{2,1,0:T(8,128)(2,1)}, f32[8,768]{1,0:T(8,128)}) custom-call(bf16[2304,1024]{1,0:T(8,128)(2,1)} %bitcast.52, bf16[768,768]{1,0:T(8,128)(2,1)} %w_q_ref.1, bf16[768,768]{1,0:T(8,128)(2,1)} %w_k_ref.1, bf16[768,768]{1,0:T(8,128)(2,1)} %w_v_ref.1, ...), custom_call_target="tpu_custom_call" | custom-call | tf_op jit(solution)/shard_map/first_backward/pallas_call | solution.py:1262
  264.1 2.2 fusion.4
  266.4 2.1 pad_maximum_fusion.1.refs_0_
  268.6 0.7 slice.100
  269.3 1.5 slice.99
  270.8 0.7 copy.47
  273.1 91.8 %tail.1 = (f32[4128,192]{1,0:T(8,128)}, f32[80,768]{1,0:T(8,128)}, f32[80,768]{1,0:T(8,128)}, bf16[1024,768]{1,0:T(8,128)(2,1)}) custom-call(bf16[4,192,1024]{2,1,0:T(8,128)(2,1)} %bitcast.53, s32[4,1,1024]{2,1,0:T(1,128)} %reshape.128.slots_ref, s32[8,1,768]{2,1,0:T(1,128)} %reshape.130.ids_ref, bf16[4,2,2,2,80,768]{5,4,3,2,1,0:T(8,128)(2,1)} %pad_maximum_fusion.1.refs_0_, ...), custom_call_target="tpu_custom_call" | custom-call | tf_op jit(solution)/shard_map/tail/pallas_call | solution.py:734
  364.9 0.7 slice.93
  365.7 1.8 fusion.5
  367.5 1.3 slice.89
  370.0 5.5 %copy.43 = f32[4128,192]{0,1:T(8,128)} copy(f32[4128,192]{1,0:T(8,128)} %get-tuple-element.77) | data formatting | bytes 6340608
  375.4 3.1 fusion.8
  378.5 1.1 copy.52
  (64 shorter events, 7.2 us)
Async XLA Ops:
  7.1 53.7 %copy-start.7 = (bf16[768,768]{1,0:T(8,128)(2,1)S(1)}, bf16[768,768]{1,0:T(8,128)(2,1)}, u32[]{:S(2)}) copy-start(bf16[768,768]{1,0:T(8,128)(2,1)} %w_q_ref.1) | copy-start | bytes 3538948
  55.6 215.9 %collective-permute-start = (s32[2560]{0:T(1024)S(1)}, s32[2560]{0:T(1024)S(1)}, u32[]{:S(2)}, u32[]{:S(2)}) collective-permute-start(s32[2560]{0:T(1024)S(1)} %pad_add_fusion.4), channel_id=1, source_target_pairs={{0,8},{8,16},{16,24},{24,0},{1,9},{9,17},{17,25},{25,1},{2,10},{10... | collective-permute-start | bytes 30728 | tf_op jit(solution)/shard_map/ppermute | solution.py:1334
  56.9 214.7 %collective-permute-start.1 = (s32[2560]{0:T(1024)S(1)}, s32[2560]{0:T(1024)S(1)}, u32[]{:S(2)}, u32[]{:S(2)}) collective-permute-start(s32[2560]{0:T(1024)S(1)} %pad_add_fusion.4), channel_id=1, source_target_pairs={{0,16},{8,24},{16,0},{24,8},{1,17},{9,25},{17,1},{25,9},{2,18},{10... | collective-permute-start | bytes 30728 | tf_op jit(solution)/shard_map/ppermute | solution.py:1334
  59.2 212.4 %collective-permute-start.2 = (s32[2560]{0:T(1024)S(1)}, s32[2560]{0:T(1024)S(1)}, u32[]{:S(2)}, u32[]{:S(2)}) collective-permute-start(s32[2560]{0:T(1024)S(1)} %pad_add_fusion.4), channel_id=1, source_target_pairs={{0,24},{8,0},{16,8},{24,16},{1,25},{9,1},{17,9},{25,17},{2,26},{10... | collective-permute-start | bytes 30728 | tf_op jit(solution)/shard_map/ppermute | solution.py:1334
  60.8 3.0 copy-start.5
  60.8 3.0 copy-start.8
  63.8 4.5 %copy-start.1 = (bf16[768,1024]{1,0:T(8,128)(2,1)}, bf16[768,1024]{1,0:T(8,128)(2,1)S(1)}, u32[]{:S(2)}) copy-start(bf16[768,1024]{1,0:T(8,128)(2,1)S(1)} %fusion.q_ref) | copy-start | bytes 4718596
  63.8 1.8 copy-start.9
  65.7 2.7 copy-start.2
  65.7 1.4 copy-start.16
  65.7 2.1 copy-start.17
  67.1 46.6 %copy-start.3 = (bf16[768,1024]{1,0:T(8,128)(2,1)}, bf16[768,1024]{1,0:T(8,128)(2,1)S(1)}, u32[]{:S(2)}) copy-start(bf16[768,1024]{1,0:T(8,128)(2,1)S(1)} %fusion.2.v_ref) | copy-start | bytes 4718596
  113.7 1.1 copy-start
  114.8 0.6 copy-start.4
  180.3 2.7 copy-start.14
  183.0 1.7 copy-start.11
  264.1 2.2 copy-start.15
  266.4 2.1 copy-start.13
  370.0 5.5 %copy-start.10 = (bf16[768,768]{1,0:T(8,128)(2,1)S(1)}, bf16[768,768]{1,0:T(8,128)(2,1)}, u32[]{:S(2)}) copy-start(bf16[768,768]{1,0:T(8,128)(2,1)} %w_patch_ref.1) | copy-start | bytes 3538948
  370.0 5.5 %copy-start.18 = (bf16[1024,768]{1,0:T(8,128)(2,1)S(1)}, bf16[1024,768]{1,0:T(8,128)(2,1)}, u32[]{:S(2)}) copy-start(bf16[1024,768]{1,0:T(8,128)(2,1)} %get-tuple-element.68) | copy-start | bytes 4718596
  375.4 3.1 copy-start.6
  378.5 1.1 copy-start.12
where the time goes:
time: 389 us; the launch traced here: 381 us
  Pallas kernels  325 us (84%)
  local copies, waits for them, and re-layouts  30 us (8%)
  other arithmetic  9.25 us (2%)
  matrix products  8.94 us (2%)
  starting transfers between devices  5.18 us (1%)
    pallas_call x1, Pallas kernels, tail(): pl.pallas_call(functools.partial(tail_kernel, inside), in_specs=[anywhere...  91.8 us
    pallas_call x1, Pallas kernels, feed(): pl.pallas_call(feed_kernel, grid=(2 * groups,), in_specs=[whole(attended)...  64.8 us
    pallas_call x1, Pallas kernels, attention_backward(): pl.pallas_call(functools.partial(backward_kernel, HEADS_STEP), grid=(head...  58.3 us
    pallas_call x1, Pallas kernels, front(): pl.pallas_call(front_kernel, in_specs=[pl.BlockSpec(memory_space=pltpu.SM...  47 us
    pallas_call x1, Pallas kernels, attention_forward(): pl.pallas_call(functools.partial(forward_kernel, HEADS_STEP), grid=(heads...  45.3 us
    pallas_call x1, Pallas kernels, first_backward(): pl.pallas_call(first_kernel, in_specs=[vmem] * 8, out_specs=[vmem] * 4, o...  18.2 us
    unnamed x41, local copies, waits for them, and re-layouts  9.55 us
    dot_general x4, matrix products, contract(): lax.dot_general(left, right, (((left_dim,), (right_dim,)), ((), ())), pre...  8.94 us
  transfers between devices with their start and end apart: 3, of which 0 were waited for; matrix products, arithmetic and copies ran while one was open for 6% of the time, Pallas kernels for 49%

commit v1 on v0

--- a/solution.py
+++ b/solution.py
@@ -121,15 +121,30 @@
     pack_one,
     pack_two,
     part_ref,
+    facts_ref,
     d_ref,
     out_one,
     out_two,
     ring_ref,
+    facts_out,
     s_ref,
     *refs,
 ):
     ring = Ring(part_ref, ring_ref, refs[:3])
-    first, second = shares_of([pack_one, pack_two], [out_one, out_two], refs[3:])
+    facts_landed, facts_send, facts_got = refs[3:6]
+    first, second = shares_of([pack_one, pack_two], [out_one, out_two], refs[6:])
+    groups = ring.groups
+
+    def tell(step):
+        return pltpu.make_async_remote_copy(
+            src_ref=facts_ref,
+            dst_ref=facts_landed.at[step - 1],
+            send_sem=facts_send.at[step - 1],
+            recv_sem=facts_got.at[step - 1],
+            device_id={"dp": lax.rem(ring.group + step, groups)},
+            device_id_type=MESH,
+        )
+
     bits = first.bits
     number = pl.program_id(0)
     last = pl.num_programs(0) - 1
@@ -140,6 +155,8 @@
         first.start()
         second.start()
         ring.start()
+        for step in range(1, groups):
+            tell(step).start()
 
     @pl.when(number == 1)
     def first_swap():
@@ -205,13 +222,17 @@
 
     @pl.when(number == last)
     def end():
+        facts_out[0] = facts_ref[...]
+        for step in range(1, groups):
+            tell(step).wait()
+            facts_out[step] = facts_landed[step - 1]
         ring.finish()
         first.finish()
         second.finish()
 
 
 def attention_backward(
-    queries, key_heads, values, attended, grads, probs, inverse, packs, part
+    queries, key_heads, values, attended, grads, probs, inverse, packs, part, facts
 ):
     width, length = queries.shape
     heads = width // HEAD_DIM
@@ -219,6 +240,9 @@
     rows = pl.BlockSpec((HEADS_STEP * HEAD_DIM, length), lambda g: (g, 0))
     scratch = [pltpu.VMEM((HEADS_STEP, packed, BLOCK), jnp.bfloat16)]
     scratch = scratch + ring_scratch(part.shape)
+    groups = part.shape[0]
+    semaphores = pltpu.SemaphoreType.DMA((groups - 1,))
+    scratch = scratch + [pltpu.VMEM((groups - 1,) + facts.shape, jnp.int32), semaphores, semaphores]
     for pack in packs:
         scratch = scratch + shares_scratch(pack.shape)
     return pl.pallas_call(
@@ -231,25 +255,28 @@
             pl.BlockSpec(memory_space=pl.ANY),
             pl.BlockSpec(memory_space=pl.ANY),
             pl.BlockSpec(part.shape, lambda g: (0, 0, 0)),
+            pl.BlockSpec(facts.shape, lambda g: (0, 0)),
         ],
         out_specs=[
             pl.BlockSpec((3, HEADS_STEP * HEAD_DIM, length), lambda g: (0, g, 0)),
             pl.BlockSpec(packs[0].shape[-2:], lambda g: (0, 0)),
             pl.BlockSpec(packs[1].shape[-2:], lambda g: (0, 0)),
             pl.BlockSpec(part.shape[-2:], lambda g: (0, 0)),
+            pl.BlockSpec((groups,) + facts.shape, lambda g: (0, 0, 0)),
         ],
         out_shape=[
             jax.ShapeDtypeStruct((3, width, length), jnp.bfloat16),
             jax.ShapeDtypeStruct(packs[0].shape[-2:], jnp.float32),
             jax.ShapeDtypeStruct(packs[1].shape[-2:], jnp.float32),
             jax.ShapeDtypeStruct(part.shape[-2:], jnp.float32),
+            jax.ShapeDtypeStruct((groups,) + facts.shape, jnp.int32),
         ],
         scratch_shapes=scratch,
         compiler_params=pltpu.CompilerParams(
             collective_id=2, has_side_effects=True, vmem_limit_bytes=56 << 20
         ),
         name="attention_backward",
-    )(queries, key_heads, values, attended, grads, probs, inverse, *packs, part)
+    )(queries, key_heads, values, attended, grads, probs, inverse, *packs, part, facts)
 
 
 def bit_of(index, bit):
@@ -1329,15 +1356,7 @@
         bias_row,
         capacity,
     )
-    facts = jnp.concatenate([ids.reshape(-1), slots.reshape(-1)])
-    ring = [facts] + [
-        lax.ppermute(facts, "dp", [(i, (i + step) % groups) for i in range(groups)])
-        for step in range(1, groups)
-    ]
-    ring = jnp.stack(ring)
-    ring_ids = ring[:, : owners_total * capacity].reshape(groups, owners_total, capacity)
-    ring_ids = jnp.swapaxes(ring_ids, 0, 1).reshape(owners_total, 1, groups * capacity)
-    ring_slots = ring[:, owners_total * capacity :].reshape(groups, 1, length)
+    facts = jnp.concatenate([ids.reshape(1, -1), slots], 1)
     queries = contract(w_q, normed_one, 0, 1).astype(jnp.bfloat16)
     key_heads = contract(w_k, normed_one, 0, 1).astype(jnp.bfloat16)
     value_heads = contract(w_v, normed_one, 0, 1).astype(jnp.bfloat16)
@@ -1360,7 +1379,7 @@
     for n in range(folds):
         pieces = [grad_w_up[n * per_fold + m] for m in range(per_fold)]
         folded.append(rows_of(jnp.concatenate(pieces, 1) if per_fold > 1 else pieces[0]))
-    grad_heads, share_one, share_two, share_down = attention_backward(
+    grad_heads, share_one, share_two, share_down, ring = attention_backward(
         queries,
         key_heads,
         value_heads,
@@ -1373,7 +1392,12 @@
             stacked(folded[2:]),
         ],
         part_down,
+        facts,
     )
+    ring = ring.reshape(groups, -1)
+    ring_ids = ring[:, : owners_total * capacity].reshape(groups, owners_total, capacity)
+    ring_ids = jnp.swapaxes(ring_ids, 0, 1).reshape(owners_total, 1, groups * capacity)
+    ring_slots = ring[:, owners_total * capacity :].reshape(groups, 1, length)
     grad_heads = grad_heads.reshape(3 * model_width, length)
     grad_embedded, grads_turned, grad_w_heads, gains = first_backward(
         grad_heads, w_q, w_k, w_v, embedded, grad_middle, normed_one, gain_row

time: 389 us -> 385 us (0.990)
  starting transfers between devices: 5.18 us -> 0 us
    ppermute x3 -> x0, starting transfers between devices: 5.18 us -> none  [on_device(): lax.ppermute(facts, 'dp', [(i, (i + step) % groups) for i in range(groups)])]
    unnamed x41 -> x46, local copies, waits for them, and re-layouts: 9.55 us -> 9.56 us
  transfers between devices with their start and end apart: 3 -> 0, of which waited for: 0 -> 0; matrix products, arithmetic and copies ran while one was open for 6% -> 0% of each run, Pallas kernels for 49% -> 0%
where the time goes in v1:
time: 385 us; the launch traced here: 378 us
  Pallas kernels  328 us (85%)
  local copies, waits for them, and re-layouts  30 us (8%)
  other arithmetic  9.3 us (2%)
  matrix products  8.96 us (2%)
    pallas_call x1, Pallas kernels, tail(): pl.pallas_call(functools.partial(tail_kernel, inside), in_specs=[anywhere...  93 us
    pallas_call x1, Pallas kernels, feed(): pl.pallas_call(feed_kernel, grid=(2 * groups,), in_specs=[whole(attended)...  64 us
    pallas_call x1, Pallas kernels, attention_backward(): pl.pallas_call(functools.partial(backward_kernel, HEADS_STEP), grid=(head...  60.1 us
    pallas_call x1, Pallas kernels, front(): pl.pallas_call(front_kernel, in_specs=[pl.BlockSpec(memory_space=pltpu.SM...  47 us
    pallas_call x1, Pallas kernels, attention_forward(): pl.pallas_call(functools.partial(forward_kernel, HEADS_STEP), grid=(heads...  45.4 us
    pallas_call x1, Pallas kernels, first_backward(): pl.pallas_call(first_kernel, in_specs=[vmem] * 8, out_specs=[vmem] * 4, o...  18.1 us
    unnamed x46, local copies, waits for them, and re-layouts  9.56 us
    dot_general x4, matrix products, contract(): lax.dot_general(left, right, (((left_dim,), (right_dim,)), ((), ())), pre...  8.96 us

profile of v1, /device:TPU:1, one launch (start us, length us, event | category | flops | bytes accessed | tf_op | source)
XLA Modules:
  0.0 377.9 jit_solution(11120003880669034363)
XLA Ops:
  0.7 1.3 fusion.7
  2.6 1.9 select_select_fusion
  4.6 1.3 reshape.134.gain_ref
  5.8 1.3 reshape.136.bias_ref
  7.1 47.0 %front.1 = (f32[1024,768]{1,0:T(8,128)}, bf16[1024,768]{1,0:T(8,128)(2,1)}, bf16[1024,768]{1,0:T(8,128)(2,1)}, bf16[1024,768]{1,0:T(8,128)(2,1)}, bf16[1024,768]...) custom-call(s32[1,2]{1,0:T(1,128)} %refs_1_.1, s32[1,1024]{1,0:T(1,128)} %bitcast.62, s32[1,1024]{1,0:T(1,128)} %bitcast.63, ...), custom_call_target="tpu_custom_call" | custom-call | tf_op jit(solution)/shard_map/front/pallas_call | solution.py:986
  54.1 3.0 fusion.q_ref
  57.2 1.4 fusion.1.k_ref
  59.0 1.4 fusion.2.v_ref
  60.5 45.4 %attention_forward.1 = (bf16[768,1024]{1,0:T(8,128)(2,1)S(1)}, bf16[24,2560,256]{2,1,0:T(8,128)(2,1)}, f32[24,1,1024]{2,1,0:T(1,128)S(1)}) custom-call(bf16[768,1024]{1,0:T(8,128)(2,1)S(1)} %fusion.q_ref, bf16[768,1024]{1,0:T(8,128)(2,1)S(1)} %fusion.1.k_ref, bf16[768,1024]{1,0:T(8,128)(2,1)S(1)} %fusion.2.v_ref), custom_call_target="tpu_custom_call" | custom-call | flops 49999998976 | bytes 31457280 | tf_op jit(solution)/shard_map/attention_forward/pallas_call | solution.py:90
  105.8 1.1 copy-done
  108.8 64.0 %feed.1 = (bf16[1024,768]{1,0:T(8,128)(2,1)}, f32[1024,768]{1,0:T(8,128)}, bf16[4,768,768]{2,1,0:T(8,128)(2,1)}, bf16[768,1024]{1,0:T(8,128)(2,1)}, bf16[768,768...) custom-call(bf16[768,1024]{1,0:T(8,128)(2,1)} %copy-done, ...), custom_call_target="tpu_custom_call" | custom-call | tf_op jit(solution)/shard_map/feed/pallas_call | solution.py:1201
  172.8 2.7 fusion.3
  175.6 2.1 pad_maximum_fusion.pack_one
  177.7 1.6 pad_maximum_fusion.2.pack_two
  180.0 60.1 %attention_backward.1 = (bf16[3,768,1024]{2,1,0:T(8,128)(2,1)}, f32[80,768]{1,0:T(8,128)}, f32[48,768]{1,0:T(8,128)}, f32[96,768]{1,0:T(8,128)}, s32[4,1,2560]{2,1,0:T(1,128)}) custom-call(bf16[768,1024]{1,0:T(8,128)(2,1)} %copy-done.1, bf16[768,1024]{1,0:T(8,128)(2,1)} %copy-done.2, bf16[768,1024]{1,0:T(8,128)(2,1)} %copy-done.3, ...), custom_call_target="tpu_custom_call" | custom-call | tf_op jit(solution)/shard_map/attention_backward/pallas_call | solution.py:248
  240.1 0.9 slice.103
  241.0 0.9 pad_maximum_fusion.3
  242.0 0.7 copy.48
  242.7 18.1 %first_backward.1 = (f32[1024,768]{1,0:T(8,128)}, bf16[768,1024]{1,0:T(8,128)(2,1)}, bf16[3,768,768]{2,1,0:T(8,128)(2,1)}, f32[8,768]{1,0:T(8,128)}) custom-call(bf16[2304,1024]{1,0:T(8,128)(2,1)} %bitcast.54, bf16[768,768]{1,0:T(8,128)(2,1)} %w_q_ref.1, bf16[768,768]{1,0:T(8,128)(2,1)} %w_k_ref.1, bf16[768,768]{1,0:T(8,128)(2,1)} %w_v_ref.1, ...), custom_call_target="tpu_custom_call" | custom-call | tf_op jit(solution)/shard_map/first_backward/pallas_call | solution.py:1289
  260.9 2.2 fusion.4
  263.1 2.1 pad_maximum_fusion.1.refs_0_
  265.4 0.7 reshape.130.ids_ref
  266.7 93.0 %tail.1 = (f32[4128,192]{1,0:T(8,128)}, f32[80,768]{1,0:T(8,128)}, f32[80,768]{1,0:T(8,128)}, bf16[1024,768]{1,0:T(8,128)(2,1)}) custom-call(bf16[4,192,1024]{2,1,0:T(8,128)(2,1)} %bitcast.55, s32[4,1,1024]{2,1,0:T(1,128)} %reshape.128.slots_ref, s32[8,1,768]{2,1,0:T(1,128)} %reshape.130.ids_ref, bf16[4,2,2,2,80,768]{5,4,3,2,1,0:T(8,128)(2,1)} %pad_maximum_fusion.1.refs_0_, ...), custom_call_target="tpu_custom_call" | custom-call | tf_op jit(solution)/shard_map/tail/pallas_call | solution.py:761
  359.7 0.7 slice.93
  360.5 0.7 slice.100
  362.3 1.8 fusion.5
  364.2 5.5 %copy.43 = f32[4128,192]{0,1:T(8,128)} copy(f32[4128,192]{1,0:T(8,128)} %get-tuple-element.79) | data formatting | bytes 6340608
  369.6 3.1 fusion.8
  372.7 1.3 slice.89
  374.1 1.5 slice.99
  375.6 1.1 copy.55
  376.7 0.7 copy.56
  (59 shorter events, 4.9 us)
Async XLA Ops:
  7.1 47.0 %copy-start.7 = (bf16[768,768]{1,0:T(8,128)(2,1)S(1)}, bf16[768,768]{1,0:T(8,128)(2,1)}, u32[]{:S(2)}) copy-start(bf16[768,768]{1,0:T(8,128)(2,1)} %w_q_ref.1) | copy-start | bytes 3538948
  54.1 3.0 copy-start.5
  54.1 3.0 copy-start.8
  57.1 3.3 copy-start.1
  57.1 1.8 copy-start.9
  59.0 1.5 copy-start.2
  60.4 45.4 %copy-start.3 = (bf16[768,1024]{1,0:T(8,128)(2,1)}, bf16[768,1024]{1,0:T(8,128)(2,1)S(1)}, u32[]{:S(2)}) copy-start(bf16[768,1024]{1,0:T(8,128)(2,1)S(1)} %fusion.2.v_ref) | copy-start | bytes 4718596
  60.5 47.2 %copy-start.18 = (bf16[768]{0:T(1024)(128)(2,1)S(1)}, bf16[768]{0:T(1024)(128)(2,1)}, u32[]{:S(2)}) copy-start(bf16[768]{0:T(1024)(128)(2,1)} %param.37) | copy-start | bytes 4612
  60.5 47.7 %copy-start.19 = (bf16[768]{0:T(1024)(128)(2,1)S(1)}, bf16[768]{0:T(1024)(128)(2,1)}, u32[]{:S(2)}) copy-start(bf16[768]{0:T(1024)(128)(2,1)} %param.38) | copy-start | bytes 4612
  105.8 1.1 copy-start
  107.0 0.6 copy-start.4
  172.8 2.8 copy-start.14
  172.8 2.8 copy-start.11
  177.7 1.7 copy-start.16
  177.7 1.8 copy-start.17
  260.9 2.2 copy-start.15
  263.1 2.1 copy-start.13
  364.2 5.5 %copy-start.10 = (bf16[768,768]{1,0:T(8,128)(2,1)S(1)}, bf16[768,768]{1,0:T(8,128)(2,1)}, u32[]{:S(2)}) copy-start(bf16[768,768]{1,0:T(8,128)(2,1)} %w_patch_ref.1) | copy-start | bytes 3538948
  364.2 5.5 %copy-start.20 = (bf16[1024,768]{1,0:T(8,128)(2,1)S(1)}, bf16[1024,768]{1,0:T(8,128)(2,1)}, u32[]{:S(2)}) copy-start(bf16[1024,768]{1,0:T(8,128)(2,1)} %get-tuple-element.70) | copy-start | bytes 4718596
  369.6 6.0 %copy-start.6 = (bf16[1024,768]{1,0:T(8,128)(2,1)S(1)}, bf16[1024,768]{1,0:T(8,128)(2,1)}, u32[]{:S(2)}) copy-start(bf16[1024,768]{1,0:T(8,128)(2,1)} %get-tuple-element.135) | copy-start | bytes 4718596
  375.6 1.1 copy-start.12
